TPU v7x, 32 devices: a whole 2x2x4 slice. The times are simulated.
32 devices in a mesh: seq: 4 (over z), head: 4 (over x, core), batch: 2 (over y).
Axes of the slice: x: 2, y: 2, z: 4, core: 2. Of those that a mesh axis runs over, the one named last changes fastest.
Arguments:
- tokens: bfloat16 [8, 1024, 1024], P('batch', 'seq'), may hold values from -6 to 6
- cotangent: bfloat16 [8, 1024, 1024], P('batch', 'seq'), may hold values from -6 to 6
- prefix: float32 [2, 64, 1024], P(None, None, 'head'), may hold values from -6 to 6
- first_moment: float32 [2, 64, 1024], P(None, None, 'head'), may hold values from -6 to 6
- second_moment: float32 [2, 64, 1024], P(None, None, 'head'), may hold values from 6.784 to 26.88
- w_qkv: bfloat16 [3, 1024, 1024], P(None, None, 'head'), may hold values from -0.1875 to 0.1875
- proj_bias: float32 [3, 1024], P(None, 'head'), may hold values from -4 to 4
- w_out: bfloat16 [1024, 1024], P('head'), may hold values from -1.5 to 1.5
- w_in: bfloat16 [1024, 4096], P(None, 'head'), may hold values from -0.1875 to 0.1875
- ffn_bias: float32 [4096], P('head'), may hold values from -4 to 4
- w_down: bfloat16 [4096, 1024], P('head'), may hold values from -0.09375 to 0.09375
- gains: float32 [2, 1024], replicated, may hold values from 0.5 to 1.5
- shifts: float32 [4, 1024], replicated, may hold values from -4 to 4
- lengths: int32 [8], P('batch'), may hold values from 32 to 1024, as said below
- key_mask: int32 [8, 1024], P('batch', 'seq'), may hold values 0 or 1
Outputs:
- layer_out: float32 [8, 1024, 1024], P('batch', 'seq')
- input_grad: float32 [8, 1024, 1024], P('batch', 'seq')
- prefix_grad: float32 [2, 64, 1024], P(None, None, 'head')
- new_prefix: float32 [2, 64, 1024], P(None, None, 'head')
- new_first: float32 [2, 64, 1024], P(None, None, 'head')
- new_second: float32 [2, 64, 1024], P(None, None, 'head')
Inputs may be any that keep to these rules, and one draw needn't show every extreme that they name: `lengths`: one sequence of every draw has the length 1024.
All inputs are finite; a program needn't handle non-finite values. No bound on the sum of `key_mask` on one device may be relied on, other than what follows from the above.
Results may differ from a plain program's by a relative error of at most 0.029.
Values may be sent and summed in bfloat16 or wider, within the bound.
A program may use at most 128 MiB of HBM per device.

v0:
```python
import jax
import jax.numpy as jnp
from jax import lax
from jax.experimental import pallas as pl
from jax.experimental.pallas import tpu as pltpu
from jax.sharding import PartitionSpec as P

HEAD_DIM = 64
STEP = 10


NEG_FILL = -1e30
NORM_EPSILON = 1e-05
BETA_ONE = 0.9
BETA_TWO = 0.95
LEARN_RATE = 0.8
WEIGHT_DECAY = 0.01
ADAM_EPSILON = 1e-08


def shifted(value, axis, steps):
    count = lax.axis_size(axis)
    pairs = [(source, (source + steps) % count) for source in range(count)]
    return lax.ppermute(value, axis, pairs)


def layer_norm(values_in, gain_row, shift_row):
    row_mean = jnp.mean(values_in, axis=-1, keepdims=True)
    centred = values_in - row_mean
    spread = jnp.mean(centred * centred, axis=-1, keepdims=True)
    return centred * lax.rsqrt(spread + NORM_EPSILON) * gain_row + shift_row


def exact_gelu(values_in):
    return jax.nn.gelu(values_in, approximate=False)


def block_scores(queries, block_keys, block_bias, score_scale):
    scores = (
        jnp.einsum("shqd,shkd->shqk", queries, block_keys, preferred_element_type=jnp.float32)
        * score_scale
    )
    return scores + block_bias.astype(jnp.float32)[:, None, None, :]


def absorb(softmax_state, queries, block_keys, block_values, block_bias, score_scale):
    row_max, row_sum, weighted = softmax_state
    scores = block_scores(queries, block_keys, block_bias, score_scale)
    new_max = jnp.maximum(row_max, jnp.max(scores, axis=-1))
    fade_factor = jnp.exp(row_max - new_max)
    exp_scores = jnp.exp(scores - new_max[..., None])
    row_sum = row_sum * fade_factor + jnp.sum(exp_scores, axis=-1)
    weighted = weighted * fade_factor[..., None] + jnp.einsum(
        "shqk,shkd->shqd",
        exp_scores.astype(jnp.bfloat16),
        block_values,
        preferred_element_type=jnp.float32,
    )
    return (new_max, row_sum, weighted)


def back_block(
    queries, grad_att, log_total, row_delta, block_keys, block_values, block_bias, score_scale
):
    scores = block_scores(queries, block_keys, block_bias, score_scale)
    probabilities = jnp.exp(scores - log_total[..., None])
    grad_probs = jnp.einsum(
        "shqd,shkd->shqk", grad_att, block_values, preferred_element_type=jnp.float32
    )
    grad_scores = (probabilities * (grad_probs - row_delta[..., None])).astype(jnp.bfloat16)
    grad_queries = (
        jnp.einsum("shqk,shkd->shqd", grad_scores, block_keys, preferred_element_type=jnp.float32)
        * score_scale
    )
    grad_keys = (
        jnp.einsum("shqk,shqd->shkd", grad_scores, queries, preferred_element_type=jnp.float32)
        * score_scale
    )
    grad_values = jnp.einsum(
        "shqk,shqd->shkd",
        probabilities.astype(jnp.bfloat16),
        grad_att,
        preferred_element_type=jnp.float32,
    )
    return (grad_queries, grad_keys, grad_values)


def general_body(
    tokens,
    cotangent,
    prefix,
    first_moment,
    second_moment,
    w_qkv,
    proj_bias,
    w_out,
    w_in,
    ffn_bias,
    w_down,
    gains,
    shifts,
    lengths,
    key_mask,
):
    seqs_dev, shard_len, model_width = tokens.shape
    row_count = seqs_dev * shard_len
    local_width = w_qkv.shape[2]
    heads_dev = local_width // HEAD_DIM
    prefix_slots = prefix.shape[1]
    score_scale = HEAD_DIM ** (-0.5)
    cycle_size = lax.axis_size("seq")
    cycle_place = lax.axis_index("seq")
    flat_tokens = tokens.reshape(row_count, model_width)
    projected = (
        jnp.einsum("td,ide->ite", flat_tokens, w_qkv, preferred_element_type=jnp.float32)
        + proj_bias[:, None, :]
    )
    by_head = (
        projected.astype(jnp.bfloat16)
        .reshape(3, seqs_dev, shard_len, heads_dev, HEAD_DIM)
        .transpose(0, 1, 3, 2, 4)
    )
    queries = by_head[0]
    own_keys = by_head[1]
    own_values = by_head[2]
    positions = cycle_place * shard_len + lax.broadcasted_iota(jnp.int32, (seqs_dev, shard_len), 1)
    live_keys = (key_mask == 1) & (positions < lengths[:, None])
    own_bias = jnp.where(live_keys, 0.0, NEG_FILL).astype(jnp.bfloat16)
    prefix_low = (
        prefix.astype(jnp.bfloat16)
        .reshape(2, prefix_slots, heads_dev, HEAD_DIM)
        .transpose(0, 2, 1, 3)
    )
    pre_scores = (
        jnp.einsum("shqd,hpd->shqp", queries, prefix_low[0], preferred_element_type=jnp.float32)
        * score_scale
    )
    row_max = jnp.max(pre_scores, axis=-1)
    exp_prefix = jnp.exp(pre_scores - row_max[..., None])
    row_sum = jnp.sum(exp_prefix, axis=-1)
    weighted = jnp.einsum(
        "shqp,hpd->shqd",
        exp_prefix.astype(jnp.bfloat16),
        prefix_low[1],
        preferred_element_type=jnp.float32,
    )

    def visit_keys(softmax_state, block_keys, block_values, block_bias):
        return absorb(softmax_state, queries, block_keys, block_values, block_bias, score_scale)

    def forward_turn(turn_index, carried):
        softmax_state, block_keys, block_values, block_bias = carried
        softmax_state = visit_keys(softmax_state, block_keys, block_values, block_bias)
        block_keys, block_values, block_bias = shifted(
            (block_keys, block_values, block_bias), "seq", 1
        )
        return (softmax_state, block_keys, block_values, block_bias)

    carried = lax.fori_loop(
        0,
        cycle_size - 1,
        forward_turn,
        ((row_max, row_sum, weighted), own_keys, own_values, own_bias),
    )
    row_max, row_sum, weighted = visit_keys(carried[0], carried[1], carried[2], carried[3])
    log_total = row_max + jnp.log(row_sum)
    attended = weighted / row_sum[..., None]
    merged = attended.astype(jnp.bfloat16).transpose(0, 2, 1, 3).reshape(row_count, local_width)
    attention = (
        lax.psum(jnp.dot(merged, w_out, preferred_element_type=jnp.float32), "head") + shifts[0]
    )
    resid_one = flat_tokens.astype(jnp.float32) + attention
    normed, norm_one_back = jax.vjp(
        lambda values_in: layer_norm(values_in, gains[0], shifts[1]), resid_one
    )
    inner_sum = (
        jnp.dot(normed.astype(jnp.bfloat16), w_in, preferred_element_type=jnp.float32) + ffn_bias
    )
    activated, gelu_back = jax.vjp(exact_gelu, inner_sum)
    feed_forward = (
        lax.psum(
            jnp.dot(activated.astype(jnp.bfloat16), w_down, preferred_element_type=jnp.float32),
            "head",
        )
        + shifts[2]
    )
    layer_value, norm_two_back = jax.vjp(
        lambda values_in: layer_norm(values_in, gains[1], shifts[3]), normed + feed_forward
    )
    contract_last = (((1,), (1,)), ((), ()))
    (grad_two,) = norm_two_back(cotangent.reshape(row_count, model_width).astype(jnp.float32))
    grad_act = lax.dot_general(
        grad_two.astype(jnp.bfloat16), w_down, contract_last, preferred_element_type=jnp.float32
    )
    (grad_inner,) = gelu_back(grad_act)
    hidden_part = lax.dot_general(
        grad_inner.astype(jnp.bfloat16), w_in, contract_last, preferred_element_type=jnp.float32
    )
    grad_normed = grad_two + lax.psum(hidden_part, "head")
    (grad_one,) = norm_one_back(grad_normed)
    grad_merged = lax.dot_general(
        grad_one.astype(jnp.bfloat16), w_out, contract_last, preferred_element_type=jnp.float32
    )
    grad_att = (
        grad_merged.astype(jnp.bfloat16)
        .reshape(seqs_dev, shard_len, heads_dev, HEAD_DIM)
        .transpose(0, 2, 1, 3)
    )
    row_delta = jnp.sum(grad_att.astype(jnp.float32) * attended, axis=-1)
    pre_probs = jnp.exp(pre_scores - log_total[..., None])
    grad_pre_probs = jnp.einsum(
        "shqd,hpd->shqp", grad_att, prefix_low[1], preferred_element_type=jnp.float32
    )
    grad_pre_scores = (pre_probs * (grad_pre_probs - row_delta[..., None])).astype(jnp.bfloat16)
    grad_query_pre = (
        jnp.einsum(
            "shqp,hpd->shqd", grad_pre_scores, prefix_low[0], preferred_element_type=jnp.float32
        )
        * score_scale
    )
    grad_pre_keys = (
        jnp.einsum("shqp,shqd->hpd", grad_pre_scores, queries, preferred_element_type=jnp.float32)
        * score_scale
    )
    grad_pre_values = jnp.einsum(
        "shqp,shqd->hpd",
        pre_probs.astype(jnp.bfloat16),
        grad_att,
        preferred_element_type=jnp.float32,
    )
    prefix_terms = (
        jnp.stack([grad_pre_keys, grad_pre_values])
        .transpose(0, 2, 1, 3)
        .reshape(2, prefix_slots, local_width)
    )
    empty_grad = jnp.zeros(queries.shape, jnp.float32)

    def back_visit(query_side, key_side):
        return back_block(
            query_side[0],
            query_side[1],
            query_side[2],
            query_side[3],
            key_side[0],
            key_side[1],
            key_side[2],
            score_scale,
        )

    own_key_side = (own_keys, own_values, own_bias)

    def query_turn(turn_index, carried):
        grad_keys, grad_values, visit_queries, visit_grad, visit_total, visit_delta, visit_sum = (
            carried
        )
        turn_queries, turn_keys, turn_values = back_visit(
            (visit_queries, visit_grad, visit_total, visit_delta), own_key_side
        )
        moved = (
            shifted(visit_queries.astype(jnp.float32), "seq", 1).astype(visit_queries.dtype),
            shifted(visit_grad.astype(jnp.float32), "seq", 1).astype(visit_grad.dtype),
            shifted(visit_total, "seq", 1),
            shifted(visit_delta, "seq", 1),
            shifted(visit_sum + turn_queries, "seq", 1),
        )
        return (grad_keys + turn_keys, grad_values + turn_values) + moved

    carried = lax.fori_loop(
        0,
        cycle_size - 1,
        query_turn,
        (empty_grad, empty_grad, queries, grad_att, log_total, row_delta, grad_query_pre),
    )
    grad_keys, grad_values, visit_queries, visit_grad, visit_total, visit_delta, visit_sum = carried
    turn_queries, turn_keys, turn_values = back_visit(
        (visit_queries, visit_grad, visit_total, visit_delta), own_key_side
    )
    grad_keys = grad_keys + turn_keys
    grad_values = grad_values + turn_values
    grad_queries = shifted(visit_sum + turn_queries, "seq", 1)
    grad_rows = (
        jnp.stack([grad_queries, grad_keys, grad_values])
        .astype(jnp.bfloat16)
        .transpose(0, 1, 3, 2, 4)
        .reshape(3, row_count, local_width)
    )
    input_part = jnp.einsum("ite,ide->td", grad_rows, w_qkv, preferred_element_type=jnp.float32)
    input_grad = grad_one + lax.psum(input_part, "head")
    prefix_grad = lax.psum(prefix_terms, ("seq", "batch"))
    new_first = BETA_ONE * first_moment + (1.0 - BETA_ONE) * prefix_grad
    new_second = BETA_TWO * second_moment + (1.0 - BETA_TWO) * prefix_grad * prefix_grad
    first_hat = new_first / (1.0 - BETA_ONE**STEP)
    second_hat = new_second / (1.0 - BETA_TWO**STEP)
    new_prefix = prefix - LEARN_RATE * (
        first_hat / (jnp.sqrt(second_hat) + ADAM_EPSILON) + WEIGHT_DECAY * prefix
    )
    layer_out = layer_value.reshape(seqs_dev, shard_len, model_width)
    return (
        layer_out,
        input_grad.reshape(seqs_dev, shard_len, model_width),
        prefix_grad,
        new_prefix,
        new_first,
        new_second,
    )


BF = jnp.bfloat16
F32 = jnp.float32
MESH = pl.DeviceIdType.MESH
AHEAD = 2


def nn(left, right):
    return jnp.dot(left, right, preferred_element_type=F32)


def nt(left, right):
    return lax.dot_general(
        left, right, (((1,), (1,)), ((), ())), preferred_element_type=F32
    )


def remote(src, dst, send, recv, device):
    return pltpu.make_async_remote_copy(
        src, dst, send, recv, device_id=device, device_id_type=MESH
    )


def rows_at(start, size, step=64):
    return pl.ds(pl.multiple_of(start, step), size)


def places():
    z = lax.axis_index("seq")
    h = lax.axis_index("head")
    y = lax.axis_index("batch")
    return z, h, y


def member(h, u):
    chip, core = h // 2, lax.rem(h, 2)
    return 2 * lax.rem(chip + u // 2, 2) + lax.rem(core + u % 2, 2)


def z_peers(z):
    return [z + 1 - 2 * lax.rem(z, 2), 3 - z, lax.rem(z + 2, 4)]


def greet(devices):
    barrier = pltpu.get_barrier_semaphore()
    for device in devices:
        pl.semaphore_signal(barrier, inc=1, device_id=device, device_id_type=MESH)
    pl.semaphore_wait(barrier, len(devices))


def lane_masks():
    lane = lax.broadcasted_iota(jnp.int32, (1, 128), 1)
    inside = [lane < HEAD_DIM, lane >= HEAD_DIM]
    spare = [lane == HEAD_DIM, lane == 0]
    return inside, spare


def layer_kernel(
    tokens,
    cot,
    w_qkv,
    w_out,
    w_in,
    w_down,
    prefix,
    proj_bias,
    ffn_bias,
    gains,
    shifts,
    lengths,
    key_mask,
    lo_all,
    ig_all,
    pre_o,
    tok,
    cotg,
    bias_s,
    bias_g,
    wq,
    wo,
    wi,
    wd,
    fb,
    q_s,
    k_s,
    v_s,
    kx,
    vtx,
    pt,
    att_loc,
    att_all,
    rl_s,
    normed_s,
    xhat_s,
    nb_s,
    acc,
    act,
    gp,
    lo_s,
    da_s,
    da_all,
    ds_pre,
    dox,
    dq_s,
    core_out,
    core_in,
    x_out,
    x_in,
    fin,
    pre_part,
    pre_land,
    pre_sum,
    loc_sem,
    out_sem,
    tok_sem,
    cot_sem,
    bias_sem,
    fb_sem,
    att_sem,
    core_sem,
    x_sem,
    y_sem,
    c1_sem,
    c2_sem,
    lower_sem,
    lo_sem,
    lox_sem,
    loc_lo_sem,
    lox_core_sem,
    da_sem,
    part_core_sem,
    part_x_sem,
    igz_sem,
    igx_sem,
    igc_sem,
    igcx_sem,
    pre_sem,
    pre2_sem,
):
    z, h, y = places()
    core = lax.rem(h, 2)
    hc, hx, hd_ = member(h, 1), member(h, 2), member(h, 3)
    dev_core, dev_x, dev_diag, dev_y = (z, hc, y), (z, hx, y), (z, hd_, y), (z, h, 1 - y)
    zs = z_peers(z)
    width = tok.shape[1]
    piece = width // 4
    slots = prefix.shape[1]
    total = 4 * width
    group = 2 * z + y
    others = [lax.rem(group + d, 8) for d in range(1, 8)]
    greet([dev_core, dev_x, dev_diag] + [(g // 2, h, lax.rem(g, 2)) for g in others])

    half = width // 2
    my_half = rows_at(core * half, half)
    tok_copies, tok_forwards = [], []
    for k, zp in enumerate(zs):
        tok_copies.append(
            remote(tokens.at[zp, my_half], tok.at[z, my_half], tok_sem.at[0, k], tok_sem.at[1, k], (zp, h, y))
        )
        tok_forwards.append(
            remote(tok.at[zp, my_half], tok.at[zp, my_half], tok_sem.at[2, k], tok_sem.at[3, k], dev_core)
        )
    for copy in tok_copies:
        copy.start()
    tok_own = pltpu.make_async_copy(tokens.at[z], tok.at[z], loc_sem.at[0])
    tok_own.start()
    wq_own = pltpu.make_async_copy(w_qkv, wq, loc_sem.at[1])
    wq_own.start()

    chunks = [(w_out, wo, w_out.shape[0] // 2, 0, w_out.shape[0] // 2)]
    deep = w_in.shape[0] // 2
    for i in range(4):
        chunks.append((w_in, wi, deep, i * (deep // 4), deep // 4))
    deep = w_down.shape[0] // 4
    for i in range(2):
        chunks.append((w_down, wd, deep, i * (deep // 2), deep // 2))
    over_x, over_y, core_x, core_y = [], [], [], []
    for i, (src, dst, deep, offset, size) in enumerate(chunks):
        mine = rows_at(y * deep + offset, size, 128)
        other = rows_at((1 - y) * deep + offset, size, 128)
        over_x.append(remote(src.at[mine], dst.at[h, mine], x_sem.at[0, i], x_sem.at[1, i], dev_x))
        over_y.append(remote(dst.at[hx, mine], dst.at[hx, mine], y_sem.at[0, i], y_sem.at[1, i], dev_y))
        core_x.append(remote(dst.at[hx, mine], dst.at[hx, mine], c1_sem.at[0, i], c1_sem.at[1, i], dev_core))
        core_y.append(remote(dst.at[hx, other], dst.at[hx, other], c2_sem.at[0, i], c2_sem.at[1, i], dev_core))
    n_chunks = len(chunks)
    base, size = w_down.shape[0] // 2, w_down.shape[0] // 8
    lower = rows_at(base + z * size, size, 128)
    lower_x = remote(w_down.at[lower], wd.at[h, lower], x_sem.at[0, 7], x_sem.at[1, 7], dev_x)
    lower_core = [remote(wd.at[hx, lower], wd.at[hx, lower], c1_sem.at[0, 7], c1_sem.at[1, 7], dev_core)]
    lower_z = []
    for k, zp in enumerate(zs):
        theirs = rows_at(base + zp * size, size, 128)
        lower_z.append(
            remote(wd.at[hx, lower], wd.at[hx, lower], lower_sem.at[0, k], lower_sem.at[1, k], (zp, h, y))
        )
        lower_core.append(
            remote(wd.at[hx, theirs], wd.at[hx, theirs], lower_sem.at[2, k], lower_sem.at[3, k], dev_core)
        )
    x_queue = [over_x[0], lower_x] + over_x[1:]
    for copy in x_queue[:AHEAD]:
        copy.start()

    def serve_x(place):
        x_queue[place].wait_recv()
        if place == 1:
            lower_core[0].start()
        else:
            i = place - 1 if place else 0
            over_y[i].start()
            core_x[i].start()
        if place + AHEAD < len(x_queue):
            x_queue[place + AHEAD].start()

    def serve_y(i):
        over_y[i].wait_recv()
        core_y[i].start()

    own_weights, core_weights = [], []
    for i, (src, dst) in enumerate(((w_out, wo), (w_in, wi), (w_down, wd))):
        own_weights.append(pltpu.make_async_copy(src, dst.at[h], loc_sem.at[2 + i]))
        core_weights.append(remote(src, dst.at[h], core_sem.at[0, i], core_sem.at[1, i], dev_core))

    spot = lax.broadcasted_iota(jnp.int32, (8, width), 1) + z * width
    for s in range(4):
        live = (jnp.broadcast_to(key_mask[s : s + 1, :], (8, width)) == 1) & (spot < lengths[s])
        bias_s[s] = jnp.where(live, 0.0, NEG_FILL)
    bias_g[z] = bias_s[z]
    bias_copies = [
        remote(bias_s.at[zp], bias_g.at[z], bias_sem.at[0, k], bias_sem.at[1, k], (zp, h, y))
        for k, zp in enumerate(zs)
    ]
    fb[h] = jnp.broadcast_to(ffn_bias[...], fb.shape[1:])
    fb_copies = [
        remote(fb.at[h], fb.at[h], fb_sem.at[0, k], fb_sem.at[1, k], device)
        for k, device in enumerate((dev_core, dev_x, dev_diag))
    ]
    for copy in bias_copies + fb_copies:
        copy.start()
    for copy in own_weights + core_weights:
        copy.start()

    my_piece = rows_at(h * piece, piece)
    cot_copies = [
        remote(cot.at[zp, my_piece], cotg.at[z], cot_sem.at[0, k], cot_sem.at[1, k], (zp, h, y))
        for k, zp in enumerate(zs)
    ]
    cot_own = pltpu.make_async_copy(cot.at[z, my_piece], cotg.at[z], loc_sem.at[5])
    cot_own.start()

    inside, spare = lane_masks()

    pk = prefix[0].astype(BF)
    pv = prefix[1].astype(BF)
    k_s[total : total + slots, :] = pk
    v_s[total : total + slots, :] = pv
    for head in range(4):
        pair, par = head // 2, head % 2
        part = pk[:, 128 * pair : 128 * pair + 128].astype(F32)
        kx[head, total : total + slots, :] = jnp.where(inside[par], part, 0.0).astype(BF)
        vtx[head, HEAD_DIM:, :] = jnp.ones((vtx.shape[1] - HEAD_DIM, vtx.shape[2]), BF)

    def project(block):
        rows = tok[block]
        for i, target in enumerate((q_s, k_s, v_s)):
            value = (nn(rows, wq[i]) + proj_bias[i : i + 1, :]).astype(BF)
            if i == 0:
                value = (value.astype(F32) * HEAD_DIM**-0.5).astype(BF)
            for j in range(4):
                target[rows_at(j * width + block * piece, piece), :] = value[piece * j : piece * j + piece]
            if i == 1:
                column = jnp.broadcast_to(bias_g[block][0:1, :], (128, width)).T
                for head in range(4):
                    pair, par = head // 2, head % 2
                    part = value[:, 128 * pair : 128 * pair + 128].astype(F32)
                    ext = jnp.where(inside[par], part, jnp.where(spare[par], column, 0.0)).astype(BF)
                    for j in range(4):
                        kx[head, rows_at(j * width + block * piece, piece), :] = ext[piece * j : piece * j + piece]

    tok_own.wait()
    wq_own.wait()
    project(z)
    serve_x(0)
    for k, zp in enumerate(zs):
        serve_x(k + 1)
        if k != 1:
            serve_y(k // 2)
        tok_copies[k].wait_recv()
        tok_forwards[k].start()
        bias_copies[k].wait_recv()
        if k == 2:
            for copy in lower_z + cot_copies:
                copy.start()
        tok_forwards[k].wait_recv()
        project(zp)

    for i in range(4):
        flipped = v_s[i * width : (i + 1) * width, :].astype(F32).T.astype(BF)
        for head in range(4):
            vtx[head, 0:HEAD_DIM, i * width : (i + 1) * width] = flipped[HEAD_DIM * head : HEAD_DIM * (head + 1)]
    flipped = v_s[total : total + slots, :].astype(F32).T.astype(BF)
    for head in range(4):
        vtx[head, 0:HEAD_DIM, total : total + slots] = flipped[HEAD_DIM * head : HEAD_DIM * (head + 1)]

    def att_copy(u):
        j = member(h, u)
        return remote(att_loc.at[j], att_all.at[h], att_sem.at[0, u], att_sem.at[1, u], (z, j, y))

    def attend(step):
        u = 3 - step
        j = member(h, u)
        outs, recips = [], []
        for head in range(4):
            pair, par = head // 2, head % 2
            part = q_s[rows_at(j * width, width, width), 128 * pair : 128 * pair + 128].astype(F32)
            ext = jnp.where(inside[par], part, jnp.where(spare[par], 1.0, 0.0)).astype(BF)
            scores = nt(kx[head], ext)
            top = jnp.max(scores, axis=0, keepdims=True)
            weight = jnp.exp(scores - top).astype(BF)
            pt[head, j] = weight
            summed = nn(vtx[head], weight)
            recip = 1.0 / summed[HEAD_DIM : HEAD_DIM + 1]
            outs.append(summed[0:HEAD_DIM] * recip)
            recips.append(jnp.broadcast_to(recip, (32, width)))
        att_loc[j] = jnp.concatenate(outs, axis=0).T.astype(BF)
        rl_s[j] = jnp.concatenate(recips, axis=0).T

        @pl.when(u > 0)
        def _():
            att_copy(u).start()

        @pl.when(u == 0)
        def _():
            att_all[h] = att_loc[h]

    pl.loop(0, 2)(attend)
    serve_x(4)
    serve_y(2)
    pl.loop(2, 4)(attend)
    serve_x(5)
    serve_y(3)
    att_copies = [att_copy(u) for u in (1, 2, 3)]

    lane = lax.broadcasted_iota(jnp.int32, (1, 128), 1)
    spare_lo = [lane == HEAD_DIM + 1, lane == 1]
    for head in range(4):
        pair, par = head // 2, head % 2
        part = v_s[:, 128 * pair : 128 * pair + 128].astype(F32)
        ones = jnp.where(spare[par] | spare_lo[par], 1.0, 0.0)
        kx[head] = jnp.where(inside[par], part, ones).astype(BF)
    for i in range(5):
        low, size = i * width, width if i < 4 else slots
        flipped = k_s[low : low + size, :].astype(F32).T.astype(BF)
        for head in range(4):
            vtx[head, 0:HEAD_DIM, low : low + size] = flipped[HEAD_DIM * head : HEAD_DIM * (head + 1)]

    own_weights[0].wait()
    core_weights[0].wait_recv()
    core_x[0].wait_recv()
    core_y[0].wait_recv()
    for copy in att_copies:
        copy.wait_recv()
    attention = nn(att_all[0], wo[0])
    for j in range(1, 4):
        attention += nn(att_all[j], wo[j])
    mine = jnp.concatenate([tok[b, my_piece, :] for b in range(4)], axis=0).astype(F32)
    resid = mine + attention + shifts[0:1, :]
    centred = resid - jnp.mean(resid, axis=-1, keepdims=True)
    inverse_one = lax.rsqrt(jnp.mean(centred * centred, axis=-1, keepdims=True) + NORM_EPSILON)
    xhat = centred * inverse_one
    xhat_s[...] = xhat
    normed = xhat * gains[0:1, :] + shifts[1:2, :]
    normed_s[...] = normed
    nb_s[...] = normed.astype(BF)

    tile = 256
    tiles = wi.shape[2] // tile

    def ffn_in(quarter):
        @pl.loop(0, tiles, unroll=4)
        def _(n):
            cols = rows_at(n * tile, tile, tile)
            inner = nn(nb_s[...], wi[quarter, :, cols]) + fb[quarter, 0:1, cols]
            cdf = 0.5 * (1.0 + lax.erf(inner * 0.7071067811865476))
            act[quarter, :, cols] = (inner * cdf).astype(BF)
            gp[quarter, :, cols] = cdf + inner * (jnp.exp(-0.5 * inner * inner) * 0.3989422804014327)

    for copy in fb_copies:
        copy.wait_recv()
    own_weights[1].wait()
    core_weights[1].wait_recv()
    ffn_in(h)
    ffn_in(hc)
    serve_x(6)
    serve_y(4)
    for i in range(1, 5):
        core_x[i].wait_recv()
        core_y[i].wait_recv()
    ffn_in(hx)
    ffn_in(hd_)

    acc[...] = jnp.zeros(acc.shape, F32)

    def ffn_out(quarter, start, deep):
        span = rows_at(start, deep, deep)

        @pl.loop(0, tiles, unroll=4)
        def _(n):
            cols = rows_at(n * tile, tile, tile)
            acc[:, cols] += nn(act[quarter, :, span], wd[quarter, span, cols])

    own_weights[2].wait()
    core_weights[2].wait_recv()
    deep = wd.shape[1]
    for k in range(3):
        lower_z[k].wait_recv()
        lower_core[k + 1].start()
    ffn_out(h, 0, deep)
    serve_x(7)
    serve_y(5)
    ffn_out(hc, 0, deep)
    ffn_out(hx, base, deep // 2)
    for copy in lower_core:
        copy.wait_recv()
    ffn_out(hd_, base, deep // 2)
    for i in (5, 6):
        core_x[i].wait_recv()
    ffn_out(hx, y * (deep // 4), deep // 4)
    ffn_out(hd_, y * (deep // 4), deep // 4)
    serve_y(6)
    ffn_out(hx, (1 - y) * (deep // 4), deep // 4)
    for i in (5, 6):
        core_y[i].wait_recv()
    ffn_out(hd_, (1 - y) * (deep // 4), deep // 4)

    resid = normed_s[...] + acc[...] + shifts[2:3, :]
    centred = resid - jnp.mean(resid, axis=-1, keepdims=True)
    inverse = lax.rsqrt(jnp.mean(centred * centred, axis=-1, keepdims=True) + NORM_EPSILON)
    xhat = centred * inverse
    lo_s[...] = (xhat * gains[1:2, :] + shifts[3:4, :]).astype(BF)
    x_piece = rows_at(hx * piece, piece)
    lo_z, lo_x, lo_core, lo_across = [], [], [], []
    blocks = zs + [z]
    for k, b in enumerate(blocks):
        rows = rows_at(b * piece, piece)
        source = lo_all.at[b, my_piece]
        if k < 3:
            lo_z.append(remote(lo_s.at[rows], lo_all.at[z, my_piece], lo_sem.at[0, k], lo_sem.at[1, k], (b, h, y)))
        else:
            source = lo_s.at[rows]
        lo_x.append(remote(source, lo_all.at[b, my_piece], lox_sem.at[0, k], lox_sem.at[1, k], dev_x))
        lo_core.append(remote(source, lo_all.at[b, my_piece], loc_lo_sem.at[0, k], loc_lo_sem.at[1, k], dev_core))
        lo_across.append(
            remote(lo_all.at[b, x_piece], lo_all.at[b, x_piece], lox_core_sem.at[0, k], lox_core_sem.at[1, k], dev_core)
        )
    lo_own = pltpu.make_async_copy(lo_s.at[rows_at(z * piece, piece)], lo_all.at[z, my_piece], out_sem.at[0])
    for copy in lo_z + [lo_x[3], lo_core[3], lo_own]:
        copy.start()

    def serve_lo(k):
        lo_z[k].wait_recv()
        lo_x[k].start()
        lo_core[k].start()

    cot_own.wait()
    for copy in cot_copies:
        copy.wait_recv()
    dy = jnp.concatenate([cotg[b] for b in range(4)], axis=0).astype(F32) * gains[1:2, :]
    g_two = inverse * (
        dy - jnp.mean(dy, axis=-1, keepdims=True) - xhat * jnp.mean(dy * xhat, axis=-1, keepdims=True)
    )
    acc[...] = g_two
    nb_s[...] = g_two.astype(BF)

    @pl.loop(0, 4)
    def _(quarter):
        @pl.loop(0, tiles, unroll=4)
        def _(n):
            cols = rows_at(n * tile, tile, tile)
            d_act = nt(nb_s[...], wd[quarter, cols, :])
            act[quarter, :, cols] = (d_act * gp[quarter, :, cols]).astype(BF)

    serve_lo(0)

    @pl.loop(0, 4)
    def _(quarter):
        @pl.loop(0, tiles, unroll=4)
        def _(n):
            cols = rows_at(n * tile, tile, tile)
            acc[:, cols] += nt(act[quarter], wi[quarter, cols, :])

    serve_lo(1)
    dy = acc[...] * gains[0:1, :]
    xhat = xhat_s[...]
    g_one = inverse_one * (
        dy - jnp.mean(dy, axis=-1, keepdims=True) - xhat * jnp.mean(dy * xhat, axis=-1, keepdims=True)
    )
    acc[...] = g_one
    low = g_one.astype(BF)
    da_copies = {}
    for u in (2, 3, 1):
        j = member(h, u)
        da_s[j] = nt(low, wo[j]).astype(BF)
        da_copies[u] = remote(da_s.at[j], da_all.at[h], da_sem.at[0, u], da_sem.at[1, u], (z, j, y))
        da_copies[u].start()
    da_all[h] = nt(low, wo[h]).astype(BF)
    for copy in over_y + core_x + core_y + lower_z + lower_core:
        copy.wait_send()

    @pl.loop(0, 4)
    def _(u):
        j = member(h, u)

        @pl.when(u > 0)
        def _():
            remote(da_s.at[j], da_all.at[h], da_sem.at[0, u], da_sem.at[1, u], (z, j, y)).wait_recv()

        grads = []
        for head in range(4):
            pair, par = head // 2, head % 2
            lanes = slice(128 * pair, 128 * pair + 128)
            d_out = da_all[j, :, lanes].astype(F32)
            recip = rl_s[j, :, 32 * head : 32 * head + 1]
            delta = recip * jnp.sum(
                jnp.where(inside[par], d_out * att_loc[j, :, lanes].astype(F32), 0.0), axis=-1, keepdims=True
            )
            high = delta.astype(BF).astype(F32)
            ext = jnp.where(spare[par], -high, jnp.where(spare_lo[par], high - delta, 0.0))
            ext = jnp.where(inside[par], d_out * recip, ext).astype(BF)
            dox[head, j] = ext
            d_probs = nt(kx[head], ext).astype(BF)
            d_scores = pt[head, j] * d_probs
            wi[head, :, rows_at(j * width, width, width)] = d_scores[0:total]
            ds_pre[head, j] = d_scores[total:]
            grads.append(nn(vtx[head, 0:HEAD_DIM, :], d_scores))
        dq_s[j] = (jnp.concatenate(grads, axis=0).T * HEAD_DIM**-0.5).astype(BF)

    serve_lo(2)

    def key_side(left, right):
        halves = []
        for pair in range(2):
            sides = []
            for par in range(2):
                head = 2 * pair + par
                value = nn(left(head, 0), right(head, 0, pair))
                for j in range(1, 4):
                    value += nn(left(head, j), right(head, j, pair))
                sides.append(value)
            halves.append(jnp.where(inside[0], sides[0], sides[1]))
        return jnp.concatenate(halves, axis=-1)

    def d_values(rows):
        return key_side(lambda head, j: pt[head, j, rows, :], lambda head, j, pair: dox[head, j])

    def d_keys(left):
        return key_side(left, lambda head, j, pair: q_s[j * width : (j + 1) * width, 128 * pair : 128 * pair + 128])

    def partial(i):
        rows = rows_at(i * width, width, width)
        dk = d_keys(lambda head, j: wi[head, rows, j * width : (j + 1) * width]).astype(BF)
        dv = d_values(rows).astype(BF)
        return nt(dq_s[i], wq[0]) + nt(dk, wq[1]) + nt(dv, wq[2])

    part_core = [
        remote(core_out.at[i], core_in.at[i], part_core_sem.at[0, i], part_core_sem.at[1, i], dev_core) for i in range(2)
    ]
    part_x = []
    for k, b in enumerate(blocks):
        rows = rows_at(b * piece, piece)
        part_x.append(remote(x_out.at[rows], x_in.at[rows], part_x_sem.at[0, k], part_x_sem.at[1, k], dev_x))

    core_out[0] = partial(hd_).astype(BF)
    part_core[0].start()
    mine = partial(hx)
    part_core[0].wait_recv()
    x_out[...] = (mine + core_in[0].astype(F32)).astype(BF)
    for copy in part_x:
        copy.start()

    pre_part[0] = d_keys(lambda head, j: ds_pre[head, j])
    pre_part[1] = d_values(pl.ds(total, slots))
    few = slots // 8
    mine_rows = rows_at(group * few, few, few)
    pre_copies, pre_back = [], []
    for d, g in enumerate(others):
        device = (g // 2, h, lax.rem(g, 2))
        pre_copies.append(
            remote(pre_part.at[:, rows_at(g * few, few, few)], pre_land.at[d], pre_sem.at[0, d], pre_sem.at[1, d], device)
        )
        pre_back.append(
            remote(pre_sum.at[:, mine_rows], pre_sum.at[:, mine_rows], pre2_sem.at[0, d], pre2_sem.at[1, d], device)
        )
    for copy in pre_copies:
        copy.start()
    for k in (3, 0, 1, 2):
        lo_x[k].wait_recv()
        lo_across[k].start()

    core_out[1] = partial(hc).astype(BF)
    part_core[1].start()
    acc[...] += partial(h)
    part_core[1].wait_recv()
    acc[...] += core_in[1].astype(F32)

    igz, igx, igc, igcx = [], [], [], []
    for k, b in enumerate(blocks):
        rows = rows_at(b * piece, piece)
        source = ig_all.at[b, my_piece]
        if k < 3:
            igz.append(remote(fin.at[rows], ig_all.at[z, my_piece], igz_sem.at[0, k], igz_sem.at[1, k], (b, h, y)))
        else:
            source = fin.at[rows]
        igx.append(remote(source, ig_all.at[b, my_piece], igx_sem.at[0, k], igx_sem.at[1, k], dev_x))
        igc.append(remote(source, ig_all.at[b, my_piece], igc_sem.at[0, k], igc_sem.at[1, k], dev_core))
        igcx.append(
            remote(ig_all.at[b, x_piece], ig_all.at[b, x_piece], igcx_sem.at[0, k], igcx_sem.at[1, k], dev_core)
        )
    ig_own = pltpu.make_async_copy(fin.at[rows_at(z * piece, piece)], ig_all.at[z, my_piece], out_sem.at[1])
    for k, b in enumerate(blocks):
        rows = rows_at(b * piece, piece)
        part_x[k].wait_recv()
        fin[rows, :] = (acc[rows, :] + x_in[rows, :].astype(F32)).astype(BF)
        if k < 3:
            igz[k].start()
        else:
            ig_own.start()
            igx[3].start()
            igc[3].start()
        if k == 1:
            for copy in pre_copies:
                copy.wait_recv()
            for i in range(2):
                term = pre_part[i, mine_rows, :]
                for d in range(7):
                    term += pre_land[d, i]
                pre_sum[i, mine_rows, :] = term
            for copy in pre_back:
                copy.start()
    for copy in lo_core + lo_across:
        copy.wait_recv()
    lo_own.wait()
    for k in range(3):
        igz[k].wait_recv()
        igx[k].start()
        igc[k].start()
    for copy in pre_back:
        copy.wait_recv()
    pre_o[...] = pre_sum[...]
    for k in (3, 0, 1, 2):
        igx[k].wait_recv()
        igcx[k].start()
    for copy in igc + igcx:
        copy.wait_recv()
    ig_own.wait()
    sent = tok_copies + tok_forwards + x_queue + core_weights + bias_copies + fb_copies + cot_copies + att_copies
    sent += lo_z + lo_x + lo_core + lo_across + list(da_copies.values()) + part_core + part_x
    for copy in sent + igz + igx + igc + igcx + pre_copies + pre_back:
        copy.wait_send()


def layer(tokens, cot, w_qkv, w_out, w_in, w_down, prefix, proj_bias, ffn_bias, gains, shifts, lengths, key_mask):
    seqs, width, model = tokens.shape
    local = w_qkv.shape[2]
    hidden = w_in.shape[1]
    slots = prefix.shape[1]
    total = seqs * width
    keys = total + slots
    dma = pltpu.SemaphoreType.DMA
    hbm = pl.BlockSpec(memory_space=pl.ANY)
    vmem = pl.BlockSpec(memory_space=pltpu.VMEM)
    shape = jax.ShapeDtypeStruct
    return pl.pallas_call(
        layer_kernel,
        name="layer",
        out_shape=(
            pltpu.VMEM((4, width, model), BF),
            pltpu.VMEM((4, width, model), BF),
            shape((2, slots, local), F32),
        ),
        in_specs=[hbm] * 6 + [vmem] * 5 + [pl.BlockSpec(memory_space=pltpu.SMEM), vmem],
        out_specs=(vmem, vmem, vmem),
        scratch_shapes=[
            pltpu.VMEM((4, width, model), BF),
            pltpu.VMEM((4, width // 4, model), BF),
            pltpu.VMEM((4, 8, width), F32),
            pltpu.VMEM((4, 8, width), F32),
            pltpu.VMEM((3, model, local), BF),
            pltpu.VMEM((4, local, model), BF),
            pltpu.VMEM((4, model, hidden), BF),
            pltpu.VMEM((4, hidden, model), BF),
            pltpu.VMEM((4, 8, hidden), F32),
            pltpu.VMEM((total, local), BF),
            pltpu.VMEM((keys, local), BF),
            pltpu.VMEM((keys, local), BF),
            pltpu.VMEM((4, keys, 128), BF),
            pltpu.VMEM((4, HEAD_DIM + 16, keys), BF),
            pltpu.VMEM((4, 4, keys, width), BF),
            pltpu.VMEM((4, width, local), BF),
            pltpu.VMEM((4, width, local), BF),
            pltpu.VMEM((4, width, 128), F32),
            pltpu.VMEM((width, model), F32),
            pltpu.VMEM((width, model), F32),
            pltpu.VMEM((width, model), BF),
            pltpu.VMEM((width, model), F32),
            pltpu.VMEM((4, width, hidden), BF),
            pltpu.VMEM((4, width, hidden), F32),
            pltpu.VMEM((width, model), BF),
            pltpu.VMEM((4, width, local), BF),
            pltpu.VMEM((4, width, local), BF),
            pltpu.VMEM((4, 4, slots, width), BF),
            pltpu.VMEM((4, 4, width, 128), BF),
            pltpu.VMEM((4, width, local), BF),
            pltpu.VMEM((2, width, model), BF),
            pltpu.VMEM((2, width, model), BF),
            pltpu.VMEM((width, model), BF),
            pltpu.VMEM((width, model), BF),
            pltpu.VMEM((width, model), BF),
            pltpu.VMEM((2, slots, local), F32),
            pltpu.VMEM((7, 2, slots // 8, local), F32),
            pltpu.VMEM((2, slots, local), F32),
            dma((6,)),
            dma((4,)),
            dma((4, 3)),
            dma((2, 3)),
            dma((2, 3)),
            dma((2, 3)),
            dma((2, 4)),
            dma((2, 3)),
            dma((2, 9)),
            dma((2, 9)),
            dma((2, 9)),
            dma((2, 9)),
            dma((4, 3)),
            dma((2, 3)),
            dma((2, 4)),
            dma((2, 4)),
            dma((2, 4)),
            dma((2, 4)),
            dma((2, 2)),
            dma((2, 4)),
            dma((2, 3)),
            dma((2, 4)),
            dma((2, 4)),
            dma((2, 4)),
            dma((2, 7)),
            dma((2, 7)),
        ],
        compiler_params=pltpu.CompilerParams(
            collective_id=0, has_side_effects=True, vmem_limit_bytes=58 * 2**20
        ),
        cost_estimate=pl.CostEstimate(flops=15 * 10**9, bytes_accessed=40 * 2**20, transcendentals=6 * 10**6),
    )(tokens, cot, w_qkv, w_out, w_in, w_down, prefix, proj_bias, ffn_bias, gains, shifts, lengths, key_mask)


def finish_kernel(lo, ig, grad, prefix, first, second, lo_o, ig_o, grad_o, new_o, first_o, second_o, lo_f, ig_f, sem):
    seqs = lo.shape[0]
    copies = []
    for i in range(seqs):
        for k, (src, mid, dst) in enumerate(((lo, lo_f, lo_o), (ig, ig_f, ig_o))):
            mid[i] = src[i].astype(F32)
            copy = pltpu.make_async_copy(mid.at[i], dst.at[i], sem.at[k, i])
            copy.start()
            copies.append(copy)
    slope = grad[...]
    grad_o[...] = slope
    new_first = BETA_ONE * first[...] + (1.0 - BETA_ONE) * slope
    new_second = BETA_TWO * second[...] + (1.0 - BETA_TWO) * slope * slope
    first_hat = new_first / (1.0 - BETA_ONE**STEP)
    second_hat = new_second / (1.0 - BETA_TWO**STEP)
    value = prefix[...]
    new_o[...] = value - LEARN_RATE * (first_hat / (jnp.sqrt(second_hat) + ADAM_EPSILON) + WEIGHT_DECAY * value)
    first_o[...] = new_first
    second_o[...] = new_second
    for copy in copies:
        copy.wait()


def finish(lo, ig, grad, prefix, first, second):
    hbm = pl.BlockSpec(memory_space=pl.ANY)
    vmem = pl.BlockSpec(memory_space=pltpu.VMEM)
    shape = jax.ShapeDtypeStruct
    whole, little = shape(lo.shape, F32), shape(prefix.shape, F32)
    return pl.pallas_call(
        finish_kernel,
        name="finish",
        out_shape=(whole, whole, little, little, little, little),
        in_specs=[vmem] * 6,
        out_specs=(hbm, hbm, vmem, vmem, vmem, vmem),
        scratch_shapes=[
            pltpu.VMEM(lo.shape, F32),
            pltpu.VMEM(lo.shape, F32),
            pltpu.SemaphoreType.DMA((2, lo.shape[0])),
        ],
        compiler_params=pltpu.CompilerParams(vmem_limit_bytes=40 * 2**20),
    )(lo, ig, grad, prefix, first, second)


def body(*args):
    (tokens, cotangent, prefix, first_moment, second_moment, w_qkv, proj_bias, w_out, w_in, ffn_bias) = args[:10]
    w_down, gains, shifts, lengths, key_mask = args[10:]
    fits = (
        lax.axis_size("seq") == 4
        and lax.axis_size("head") == 4
        and lax.axis_size("batch") == 2
        and tokens.shape == (4, 256, 1024)
        and w_qkv.shape == (3, 1024, 256)
        and w_in.shape == (1024, 1024)
        and prefix.shape[1] == 64
    )
    if not fits:
        return general_body(*args)
    layer_out, input_grad, prefix_grad = layer(
        tokens, cotangent, w_qkv, w_out, w_in, w_down, prefix, proj_bias, ffn_bias.reshape(1, -1), gains, shifts,
        lengths, key_mask,
    )
    layer_out, input_grad, prefix_grad, new_prefix, new_first, new_second = finish(
        layer_out, input_grad, prefix_grad, prefix, first_moment, second_moment
    )
    return layer_out, input_grad, prefix_grad, new_prefix, new_first, new_second


def solution(mesh):
    placed = (
        P("batch", "seq", None),
        P("batch", "seq", None),
        P(None, None, "head"),
        P(None, None, "head"),
        P(None, None, "head"),
        P(None, None, "head"),
        P(None, "head"),
        P("head", None),
        P(None, "head"),
        P("head"),
        P("head", None),
        P(),
        P(),
        P("batch"),
        P("batch", "seq"),
    )
    return jax.shard_map(
        body,
        mesh=mesh,
        in_specs=placed,
        out_specs=(
            P("batch", "seq", None),
            P("batch", "seq", None),
            P(None, None, "head"),
            P(None, None, "head"),
            P(None, None, "head"),
            P(None, None, "head"),
        ),
        check_vma=False,
    )
```

profile of v0, /device:TPU:0, one launch (start us, length us, event | category | flops | bytes accessed | tf_op | source)
XLA Modules:
  0.0 133.3 jit_solution(13345037030286133138)
XLA Ops:
  0.6 0.0 copy-start
  0.6 0.0 copy-start.1
  0.7 0.0 copy-start.2
  0.7 127.3 %layer.1 = (bf16[4,256,1024]{2,1,0:T(8,128)(2,1)S(1)}, bf16[4,256,1024]{2,1,0:T(8,128)(2,1)S(1)}, f32[2,64,256]{2,1,0:T(8,128)}) custom-call(bf16[4,256,1024]{2,1,0:T(8,128)(2,1)} %tokens.1, bf16[4,256,1024]{2,1,0:T(8,128)(2,1)} %cot.1, bf16[3,1024,256]{2,1,0:T(8,128)(2,1)} %w_qkv.1, bf16[256,1024]{1,0:T(8,128)(2,1)} %w_out.1, bf16[1024,1024]{1,0:T(8,128)(2,1)} %w_in.1, ...), custom_call_target="tpu_custom_call" | custom-call | flops 15000000512 | bytes 41943040 | tf_op jit(solution)/shard_map/layer/pallas_call | solution.py:978
  128.0 0.0 copy-done
  128.0 0.0 copy-done.1
  128.0 0.0 copy-done.2
  128.0 0.0 copy-start.3
  128.0 0.9 copy-done.3
  128.9 4.2 %finish.1 = (f32[4,256,1024]{2,1,0:T(8,128)}, f32[4,256,1024]{2,1,0:T(8,128)}, f32[2,64,256]{2,1,0:T(8,128)}, f32[2,64,256]{2,1,0:T(8,128)}, f32[2,64,256]{2,1,0:T(8,128)}, /*index=5*/f32[2,64,256]{2,1,0:T(8,128)}) custom-call(bf16[4,256,1024]{2,1,0:T(8,128)(2,1)S(1)} %get-tuple-element.9.lo, bf16[4,256,1024]{2,1,0:T(8,128)(2,1)S(1)} %get-tuple-element.10.ig, ...), custom_call_target="tpu_custom_call" | custom-call | tf_op jit(solution)/shard_map/finish/pallas_call | solution.py:1089
Async XLA Ops:
  0.6 127.4 %copy-start = (f32[2,64,256]{2,1,0:T(8,128)S(1)}, f32[2,64,256]{2,1,0:T(8,128)}, u32[]{:S(2)}) copy-start(f32[2,64,256]{2,1,0:T(8,128)} %prefix.3) | copy-start | bytes 393220
  0.6 127.4 %copy-start.1 = (f32[2,64,256]{2,1,0:T(8,128)S(1)}, f32[2,64,256]{2,1,0:T(8,128)}, u32[]{:S(2)}) copy-start(f32[2,64,256]{2,1,0:T(8,128)} %first.1) | copy-start | bytes 393220
  0.7 127.4 %copy-start.2 = (f32[2,64,256]{2,1,0:T(8,128)S(1)}, f32[2,64,256]{2,1,0:T(8,128)}, u32[]{:S(2)}) copy-start(f32[2,64,256]{2,1,0:T(8,128)} %second.1) | copy-start | bytes 393220
  128.0 0.9 copy-start.3
where the time goes:
time: 133 us
  Pallas kernels  132 us (99%)
    pallas_call x1, Pallas kernels, layer(): pl.pallas_call(layer_kernel, name='layer', out_shape=(pltpu.VMEM((4, widt...  127 us
    pallas_call x1, Pallas kernels, finish(): pl.pallas_call(finish_kernel, name='finish', out_shape=(whole, whole, lit...  4.22 us

commit v1 on v0

--- a/solution.py
+++ b/solution.py
@@ -785,8 +785,6 @@
             d_act = nt(nb_s[...], wd[quarter, cols, :])
             act[quarter, :, cols] = (d_act * gp[quarter, :, cols]).astype(BF)
 
-    serve_lo(0)
-
     @pl.loop(0, 4)
     def _(quarter):
         @pl.loop(0, tiles, unroll=4)
@@ -794,7 +792,6 @@
             cols = rows_at(n * tile, tile, tile)
             acc[:, cols] += nt(act[quarter], wi[quarter, cols, :])
 
-    serve_lo(1)
     dy = acc[...] * gains[0:1, :]
     xhat = xhat_s[...]
     g_one = inverse_one * (
@@ -812,8 +809,7 @@
     for copy in over_y + core_x + core_y + lower_z + lower_core:
         copy.wait_send()
 
-    @pl.loop(0, 4)
-    def _(u):
+    def score_grads(u):
         j = member(h, u)
 
         @pl.when(u > 0)
@@ -840,7 +836,11 @@
             grads.append(nn(vtx[head, 0:HEAD_DIM, :], d_scores))
         dq_s[j] = (jnp.concatenate(grads, axis=0).T * HEAD_DIM**-0.5).astype(BF)
 
+    pl.loop(0, 2)(score_grads)
+    serve_lo(0)
+    serve_lo(1)
     serve_lo(2)
+    pl.loop(2, 4)(score_grads)
 
     def key_side(left, right):
         halves = []

time: 133 us -> 130 us (0.977)
  Pallas kernels: 132 us -> 128 us
    pallas_call x1, Pallas kernels: 127 us -> 124 us  [layer(): pl.pallas_call(layer_kernel, name='layer', out_shape=(pltpu.VMEM((4, widt...]
where the time goes in v1:
time: 130 us
  Pallas kernels  128 us (98%)
    pallas_call x1, Pallas kernels, layer(): pl.pallas_call(layer_kernel, name='layer', out_shape=(pltpu.VMEM((4, widt...  124 us
    pallas_call x1, Pallas kernels, finish(): pl.pallas_call(finish_kernel, name='finish', out_shape=(whole, whole, lit...  4.22 us

profile of v1, /device:TPU:0, one launch (start us, length us, event | category | flops | bytes accessed | tf_op | source)
XLA Modules:
  0.0 129.5 jit_solution(7255662846183099433)
XLA Ops:
  0.6 0.0 copy-start
  0.6 0.0 copy-start.1
  0.7 0.0 copy-start.2
  0.7 123.5 %layer.1 = (bf16[4,256,1024]{2,1,0:T(8,128)(2,1)S(1)}, bf16[4,256,1024]{2,1,0:T(8,128)(2,1)S(1)}, f32[2,64,256]{2,1,0:T(8,128)}) custom-call(bf16[4,256,1024]{2,1,0:T(8,128)(2,1)} %tokens.1, bf16[4,256,1024]{2,1,0:T(8,128)(2,1)} %cot.1, bf16[3,1024,256]{2,1,0:T(8,128)(2,1)} %w_qkv.1, bf16[256,1024]{1,0:T(8,128)(2,1)} %w_out.1, bf16[1024,1024]{1,0:T(8,128)(2,1)} %w_in.1, ...), custom_call_target="tpu_custom_call" | custom-call | flops 15000000512 | bytes 41943040 | tf_op jit(solution)/shard_map/layer/pallas_call | solution.py:978
  124.2 0.0 copy-done
  124.2 0.0 copy-done.1
  124.2 0.0 copy-done.2
  124.2 0.0 copy-start.3
  124.2 0.9 copy-done.3
  125.1 4.2 %finish.1 = (f32[4,256,1024]{2,1,0:T(8,128)}, f32[4,256,1024]{2,1,0:T(8,128)}, f32[2,64,256]{2,1,0:T(8,128)}, f32[2,64,256]{2,1,0:T(8,128)}, f32[2,64,256]{2,1,0:T(8,128)}, /*index=5*/f32[2,64,256]{2,1,0:T(8,128)}) custom-call(bf16[4,256,1024]{2,1,0:T(8,128)(2,1)S(1)} %get-tuple-element.9.lo, bf16[4,256,1024]{2,1,0:T(8,128)(2,1)S(1)} %get-tuple-element.10.ig, ...), custom_call_target="tpu_custom_call" | custom-call | tf_op jit(solution)/shard_map/finish/pallas_call | solution.py:1089
Async XLA Ops:
  0.6 123.6 %copy-start = (f32[2,64,256]{2,1,0:T(8,128)S(1)}, f32[2,64,256]{2,1,0:T(8,128)}, u32[]{:S(2)}) copy-start(f32[2,64,256]{2,1,0:T(8,128)} %prefix.3) | copy-start | bytes 393220
  0.6 123.6 %copy-start.1 = (f32[2,64,256]{2,1,0:T(8,128)S(1)}, f32[2,64,256]{2,1,0:T(8,128)}, u32[]{:S(2)}) copy-start(f32[2,64,256]{2,1,0:T(8,128)} %first.1) | copy-start | bytes 393220
  0.7 123.6 %copy-start.2 = (f32[2,64,256]{2,1,0:T(8,128)S(1)}, f32[2,64,256]{2,1,0:T(8,128)}, u32[]{:S(2)}) copy-start(f32[2,64,256]{2,1,0:T(8,128)} %second.1) | copy-start | bytes 393220
  124.2 0.9 copy-start.3

commit v2 on v1

--- a/solution.py
+++ b/solution.py
@@ -478,12 +478,12 @@
     for i in range(4):
         chunks.append((w_in, wi, deep, i * (deep // 4), deep // 4))
     deep = w_down.shape[0] // 4
-    for i in range(2):
-        chunks.append((w_down, wd, deep, i * (deep // 2), deep // 2))
+    for i in range(4):
+        chunks.append((w_down, wd, deep, i * (deep // 4), deep // 4))
     over_x, over_y, core_x, core_y = [], [], [], []
     for i, (src, dst, deep, offset, size) in enumerate(chunks):
-        mine = rows_at(y * deep + offset, size, 128)
-        other = rows_at((1 - y) * deep + offset, size, 128)
+        mine = rows_at(y * deep + offset, size)
+        other = rows_at((1 - y) * deep + offset, size)
         over_x.append(remote(src.at[mine], dst.at[h, mine], x_sem.at[0, i], x_sem.at[1, i], dev_x))
         over_y.append(remote(dst.at[hx, mine], dst.at[hx, mine], y_sem.at[0, i], y_sem.at[1, i], dev_y))
         core_x.append(remote(dst.at[hx, mine], dst.at[hx, mine], c1_sem.at[0, i], c1_sem.at[1, i], dev_core))
@@ -491,8 +491,10 @@
     n_chunks = len(chunks)
     base, size = w_down.shape[0] // 2, w_down.shape[0] // 8
     lower = rows_at(base + z * size, size, 128)
-    lower_x = remote(w_down.at[lower], wd.at[h, lower], x_sem.at[0, 7], x_sem.at[1, 7], dev_x)
-    lower_core = [remote(wd.at[hx, lower], wd.at[hx, lower], c1_sem.at[0, 7], c1_sem.at[1, 7], dev_core)]
+    part = rows_at(base + z * size + y * (size // 2), size // 2)
+    lower_x = remote(w_down.at[part], wd.at[h, part], x_sem.at[0, 9], x_sem.at[1, 9], dev_x)
+    lower_y = remote(wd.at[hx, part], wd.at[hx, part], y_sem.at[0, 9], y_sem.at[1, 9], dev_y)
+    lower_core = [remote(wd.at[hx, lower], wd.at[hx, lower], c1_sem.at[0, 9], c1_sem.at[1, 9], dev_core)]
     lower_z = []
     for k, zp in enumerate(zs):
         theirs = rows_at(base + zp * size, size, 128)
@@ -509,7 +511,7 @@
     def serve_x(place):
         x_queue[place].wait_recv()
         if place == 1:
-            lower_core[0].start()
+            lower_y.start()
         else:
             i = place - 1 if place else 0
             over_y[i].start()
@@ -594,7 +596,8 @@
         tok_forwards[k].start()
         bias_copies[k].wait_recv()
         if k == 2:
-            for copy in lower_z + cot_copies:
+            lower_y.wait_recv()
+            for copy in lower_core[:1] + lower_z + cot_copies:
                 copy.start()
         tok_forwards[k].wait_recv()
         project(zp)
@@ -659,6 +662,8 @@
         for head in range(4):
             vtx[head, 0:HEAD_DIM, low : low + size] = flipped[HEAD_DIM * head : HEAD_DIM * (head + 1)]
 
+    serve_x(6)
+
     own_weights[0].wait()
     core_weights[0].wait_recv()
     core_x[0].wait_recv()
@@ -695,9 +700,10 @@
     own_weights[1].wait()
     core_weights[1].wait_recv()
     ffn_in(h)
+    serve_x(7)
     ffn_in(hc)
-    serve_x(6)
     serve_y(4)
+    serve_x(8)
     for i in range(1, 5):
         core_x[i].wait_recv()
         core_y[i].wait_recv()
@@ -721,20 +727,22 @@
         lower_z[k].wait_recv()
         lower_core[k + 1].start()
     ffn_out(h, 0, deep)
-    serve_x(7)
+    serve_x(9)
     serve_y(5)
+    serve_y(6)
     ffn_out(hc, 0, deep)
+    serve_y(7)
     ffn_out(hx, base, deep // 2)
     for copy in lower_core:
         copy.wait_recv()
     ffn_out(hd_, base, deep // 2)
-    for i in (5, 6):
+    for i in range(5, 9):
         core_x[i].wait_recv()
     ffn_out(hx, y * (deep // 4), deep // 4)
     ffn_out(hd_, y * (deep // 4), deep // 4)
-    serve_y(6)
+    serve_y(8)
     ffn_out(hx, (1 - y) * (deep // 4), deep // 4)
-    for i in (5, 6):
+    for i in range(5, 9):
         core_y[i].wait_recv()
     ffn_out(hd_, (1 - y) * (deep // 4), deep // 4)
 
@@ -806,7 +814,7 @@
         da_copies[u] = remote(da_s.at[j], da_all.at[h], da_sem.at[0, u], da_sem.at[1, u], (z, j, y))
         da_copies[u].start()
     da_all[h] = nt(low, wo[h]).astype(BF)
-    for copy in over_y + core_x + core_y + lower_z + lower_core:
+    for copy in over_y + [lower_y] + core_x + core_y + lower_z + lower_core:
         copy.wait_send()
 
     def score_grads(u):
@@ -981,7 +989,7 @@
         out_shape=(
             pltpu.VMEM((4, width, model), BF),
             pltpu.VMEM((4, width, model), BF),
-            shape((2, slots, local), F32),
+            pltpu.VMEM((2, slots, local), F32),
         ),
         in_specs=[hbm] * 6 + [vmem] * 5 + [pl.BlockSpec(memory_space=pltpu.SMEM), vmem],
         out_specs=(vmem, vmem, vmem),
@@ -1032,10 +1040,10 @@
             dma((2, 3)),
             dma((2, 4)),
             dma((2, 3)),
-            dma((2, 9)),
-            dma((2, 9)),
-            dma((2, 9)),
-            dma((2, 9)),
+            dma((2, 10)),
+            dma((2, 10)),
+            dma((2, 10)),
+            dma((2, 10)),
             dma((4, 3)),
             dma((2, 3)),
             dma((2, 4)),

time: 130 us -> 127 us (0.977)
  Pallas kernels: 128 us -> 125 us
    pallas_call x1, Pallas kernels: 124 us -> 121 us  [layer(): pl.pallas_call(layer_kernel, name='layer', out_shape=(pltpu.VMEM((4, widt...]
where the time goes in v2:
time: 127 us; the launch traced here: 126 us
  Pallas kernels  125 us (98%)
    pallas_call x1, Pallas kernels, layer(): pl.pallas_call(layer_kernel, name='layer', out_shape=(pltpu.VMEM((4, widt...  121 us
    pallas_call x1, Pallas kernels, finish(): pl.pallas_call(finish_kernel, name='finish', out_shape=(whole, whole, lit...  4.22 us

profile of v2, /device:TPU:0, one launch (start us, length us, event | category | flops | bytes accessed | tf_op | source)
XLA Modules:
  0.0 126.3 jit_solution(4898943268810035318)
XLA Ops:
  0.6 0.0 copy-start
  0.6 0.0 copy-start.1
  0.7 0.0 copy-start.2
  0.7 121.2 %layer.1 = (bf16[4,256,1024]{2,1,0:T(8,128)(2,1)S(1)}, bf16[4,256,1024]{2,1,0:T(8,128)(2,1)S(1)}, f32[2,64,256]{2,1,0:T(8,128)S(1)}) custom-call(bf16[4,256,1024]{2,1,0:T(8,128)(2,1)} %tokens.1, bf16[4,256,1024]{2,1,0:T(8,128)(2,1)} %cot.1, bf16[3,1024,256]{2,1,0:T(8,128)(2,1)} %w_qkv.1, bf16[256,1024]{1,0:T(8,128)(2,1)} %w_out.1, bf16[1024,1024]{1,0:T(8,128)(2,1)} %w_in.1, ...), custom_call_target="tpu_custom_call" | custom-call | flops 15000000512 | bytes 41943040 | tf_op jit(solution)/shard_map/layer/pallas_call | solution.py:986
  121.9 0.0 copy-done
  121.9 0.0 copy-done.1
  121.9 0.0 copy-done.2
  121.9 4.2 %finish.1 = (f32[4,256,1024]{2,1,0:T(8,128)}, f32[4,256,1024]{2,1,0:T(8,128)}, f32[2,64,256]{2,1,0:T(8,128)}, f32[2,64,256]{2,1,0:T(8,128)}, f32[2,64,256]{2,1,0:T(8,128)}, /*index=5*/f32[2,64,256]{2,1,0:T(8,128)}) custom-call(bf16[4,256,1024]{2,1,0:T(8,128)(2,1)S(1)} %get-tuple-element.9.lo, bf16[4,256,1024]{2,1,0:T(8,128)(2,1)S(1)} %get-tuple-element.10.ig, ...), custom_call_target="tpu_custom_call" | custom-call | tf_op jit(solution)/shard_map/finish/pallas_call | solution.py:1097
Async XLA Ops:
  0.6 121.3 %copy-start = (f32[2,64,256]{2,1,0:T(8,128)S(1)}, f32[2,64,256]{2,1,0:T(8,128)}, u32[]{:S(2)}) copy-start(f32[2,64,256]{2,1,0:T(8,128)} %prefix.3) | copy-start | bytes 393220
  0.6 121.3 %copy-start.1 = (f32[2,64,256]{2,1,0:T(8,128)S(1)}, f32[2,64,256]{2,1,0:T(8,128)}, u32[]{:S(2)}) copy-start(f32[2,64,256]{2,1,0:T(8,128)} %first.1) | copy-start | bytes 393220
  0.7 121.3 %copy-start.2 = (f32[2,64,256]{2,1,0:T(8,128)S(1)}, f32[2,64,256]{2,1,0:T(8,128)}, u32[]{:S(2)}) copy-start(f32[2,64,256]{2,1,0:T(8,128)} %second.1) | copy-start | bytes 393220

commit v3 on v2

--- a/solution.py
+++ b/solution.py
@@ -785,7 +785,7 @@
     acc[...] = g_two
     nb_s[...] = g_two.astype(BF)
 
-    @pl.loop(0, 4)
+    @pl.loop(0, 4, unroll=4)
     def _(quarter):
         @pl.loop(0, tiles, unroll=4)
         def _(n):
@@ -793,7 +793,7 @@
             d_act = nt(nb_s[...], wd[quarter, cols, :])
             act[quarter, :, cols] = (d_act * gp[quarter, :, cols]).astype(BF)
 
-    @pl.loop(0, 4)
+    @pl.loop(0, 4, unroll=4)
     def _(quarter):
         @pl.loop(0, tiles, unroll=4)
         def _(n):

time: 127 us -> 125 us (0.984)
    pallas_call x1, Pallas kernels: 121 us -> 120 us  [layer(): pl.pallas_call(layer_kernel, name='layer', out_shape=(pltpu.VMEM((4, widt...]
where the time goes in v3:
time: 125 us
  Pallas kernels  124 us (99%)
    pallas_call x1, Pallas kernels, layer(): pl.pallas_call(layer_kernel, name='layer', out_shape=(pltpu.VMEM((4, widt...  120 us
    pallas_call x1, Pallas kernels, finish(): pl.pallas_call(finish_kernel, name='finish', out_shape=(whole, whole, lit...  4.22 us

profile of v3, /device:TPU:0, one launch (start us, length us, event | category | flops | bytes accessed | tf_op | source)
XLA Modules:
  0.0 125.0 jit_solution(7101341338404033936)
XLA Ops:
  0.6 0.0 copy-start
  0.6 0.0 copy-start.1
  0.7 0.0 copy-start.2
  0.7 119.9 %layer.1 = (bf16[4,256,1024]{2,1,0:T(8,128)(2,1)S(1)}, bf16[4,256,1024]{2,1,0:T(8,128)(2,1)S(1)}, f32[2,64,256]{2,1,0:T(8,128)S(1)}) custom-call(bf16[4,256,1024]{2,1,0:T(8,128)(2,1)} %tokens.1, bf16[4,256,1024]{2,1,0:T(8,128)(2,1)} %cot.1, bf16[3,1024,256]{2,1,0:T(8,128)(2,1)} %w_qkv.1, bf16[256,1024]{1,0:T(8,128)(2,1)} %w_out.1, bf16[1024,1024]{1,0:T(8,128)(2,1)} %w_in.1, ...), custom_call_target="tpu_custom_call" | custom-call | flops 15000000512 | bytes 41943040 | tf_op jit(solution)/shard_map/layer/pallas_call | solution.py:986
  120.6 0.0 copy-done
  120.6 0.0 copy-done.1
  120.6 0.0 copy-done.2
  120.6 4.2 %finish.1 = (f32[4,256,1024]{2,1,0:T(8,128)}, f32[4,256,1024]{2,1,0:T(8,128)}, f32[2,64,256]{2,1,0:T(8,128)}, f32[2,64,256]{2,1,0:T(8,128)}, f32[2,64,256]{2,1,0:T(8,128)}, /*index=5*/f32[2,64,256]{2,1,0:T(8,128)}) custom-call(bf16[4,256,1024]{2,1,0:T(8,128)(2,1)S(1)} %get-tuple-element.9.lo, bf16[4,256,1024]{2,1,0:T(8,128)(2,1)S(1)} %get-tuple-element.10.ig, ...), custom_call_target="tpu_custom_call" | custom-call | tf_op jit(solution)/shard_map/finish/pallas_call | solution.py:1097
Async XLA Ops:
  0.6 119.9 %copy-start = (f32[2,64,256]{2,1,0:T(8,128)S(1)}, f32[2,64,256]{2,1,0:T(8,128)}, u32[]{:S(2)}) copy-start(f32[2,64,256]{2,1,0:T(8,128)} %prefix.3) | copy-start | bytes 393220
  0.6 119.9 %copy-start.1 = (f32[2,64,256]{2,1,0:T(8,128)S(1)}, f32[2,64,256]{2,1,0:T(8,128)}, u32[]{:S(2)}) copy-start(f32[2,64,256]{2,1,0:T(8,128)} %first.1) | copy-start | bytes 393220
  0.7 119.9 %copy-start.2 = (f32[2,64,256]{2,1,0:T(8,128)S(1)}, f32[2,64,256]{2,1,0:T(8,128)}, u32[]{:S(2)}) copy-start(f32[2,64,256]{2,1,0:T(8,128)} %second.1) | copy-start | bytes 393220
